TPU v7x, 32 devices: a whole 2x2x4 slice. The times are simulated.
32 devices in a mesh: atom: 8 (over z, core), energy: 4 (over y, x).
Axes of the slice: x: 2, y: 2, z: 4, core: 2. Of those that a mesh axis runs over, the one named last changes fastest.
Arguments:
- green: bfloat16 [64, 200, 512], P('atom', None, 'energy'), may hold values from -6 to 6
- coupling: bfloat16 [128, 800], P('atom'), may hold values from -0.625 to 0.625
- pairs: int32 [128, 2], P('atom'), may hold values from 0 to 63, as said below
- counts: int32 [8], P('atom'), may hold values from 8 to 16, as said below
- occupation: float32 [8], replicated, may hold values from 0.05 to 2
- offsets: int32 [8], replicated, may hold values from 1 to 64, as said below
Outputs:
- sigma: bfloat16 [64, 200, 512], P('atom', None, 'energy')
Inputs may be any that keep to these rules, and one draw needn't show every extreme that they name: `pairs`: slot s lies in partition p = s // 16; its first atom is one of partition p, atoms p * 8 to (p + 1) * 8 - 1. Its second atom is another atom of partition p, or one of the first 2 atoms of partition p + 1 (then its first atom is one of the last 2 atoms of partition p), or one of the last 2 atoms of partition p - 1 (then its first atom is one of the first 2 atoms of partition p); in every partition that has such a neighbour some live slot bonds to the farthest of those 2 atoms. `counts`: some partition has all its slots live. `offsets`: some mode has the largest offset.
All inputs are finite; a program needn't handle non-finite values.
Results may differ from a plain program's by a relative error of at most 0.012.
Values may be sent and summed in bfloat16 or wider, within the bound.
A program may use at most 192 MiB of HBM per device.

v0:
```python
import functools

import jax
import jax.numpy as jnp
from jax import lax
from jax.experimental import pallas as pl
from jax.experimental.pallas import tpu as pltpu
from jax.sharding import PartitionSpec as P

NORB = 10
MODES = 8
KMAX = 64
SQ = NORB * NORB
PADROW = 16
KR = NORB * PADROW
ATOMS_DEV = 8
E_DEV = 128
SLOTS = 16
MESH = pl.DeviceIdType.MESH
F32 = jnp.float32
BF16 = jnp.bfloat16
UNROLL = 4


def fill_tables(tables):
    row = lax.broadcasted_iota(jnp.int32, (SQ, 128), 0)
    lane = lax.broadcasted_iota(jnp.int32, (SQ, 128), 1)
    j = lax.shift_right_logical(lane * 205, 11)
    k = lane - j * NORB
    inside = lane < SQ
    for i in range(NORB):
        for table, want in enumerate((i * NORB + j, i * NORB + k, j * NORB + i, k * NORB + i)):
            tables[table, :, i * 128 : (i + 1) * 128] = one_where(inside & (row == want))


def one_where(mask):
    return jnp.where(mask, 1.0, 0.0).astype(BF16)


def spread_matrix():
    row = lax.broadcasted_iota(jnp.int32, (256, 2 * SQ), 0)
    col = lax.broadcasted_iota(jnp.int32, (256, 2 * SQ), 1)
    first = (row < SQ) & (col == row)
    second = (row >= 128) & (row < 128 + SQ) & (col == row - 128 + SQ)
    return one_where(first | second)


def collect_matrix():
    row = lax.broadcasted_iota(jnp.int32, (2 * SQ, 2 * KR), 0)
    col = lax.broadcasted_iota(jnp.int32, (2 * SQ, 2 * KR), 1)
    part = jnp.where(col < KR, 0, 1)
    at = col - part * KR
    i, l = lax.shift_right_logical(at, 4), at & (PADROW - 1)
    return one_where((l < NORB) & (row == part * SQ + i * NORB + l))


def term_list(own, below, above, base):
    lane = lax.broadcasted_iota(jnp.int32, (1, 128), 1).astype(F32)

    def place(rel):
        inner = jnp.where((rel == 4) | (rel == 5), rel + 4, rel)
        return jnp.where(rel < 0, rel + 12, jnp.where(rel > 7, rel - 4, inner))

    entries = []
    for group, source in ((0, own), (2, below), (3, above)):
        a, b = source[0:1] - base, source[1:2] - base
        live = lane < source[2:3, 0:1]
        if group == 0:
            entries.append((live, lane, place(b), a))
            group = 1
        entries.append((live & (b >= 0) & (b < 8), group * SLOTS + lane, place(a), b))

    before = one_where(
        lax.broadcasted_iota(jnp.int32, (128, 128), 0) < lax.broadcasted_iota(jnp.int32, (128, 128), 1)
    )
    place_at = lax.broadcasted_iota(jnp.int32, (128, 128), 0).astype(F32)
    total = jnp.zeros((1, 1), F32)
    tables = [jnp.zeros((128, 128), F32) for _ in range(3)]
    for keep, *values in entries:
        flags = jnp.where(keep, 1.0, 0.0)
        many = jnp.broadcast_to(flags, (8, 128)).astype(BF16)
        at = jnp.dot(many, before, preferred_element_type=F32)[0:1] + total
        total = total + jnp.sum(flags, axis=1, keepdims=True)
        chosen = jnp.where(place_at == at, 1.0, 0.0) * flags
        tables = [table + chosen * value for table, value in zip(tables, values)]
    ones = jnp.ones((8, 128), BF16)
    t, d, o = (
        lax.dot_general(ones, table.astype(BF16), (((1,), (1,)), ((), ())), preferred_element_type=F32)
        for table in tables
    )
    row = lax.broadcasted_iota(jnp.int32, (8, 128), 0)
    index = lax.broadcasted_iota(jnp.int32, (8, 128), 1).astype(F32)
    o = jnp.where(index < total, o, float(ATOMS_DEV))
    out = jnp.where(row == 0, t, jnp.where(row == 1, d, jnp.where(row == 2, o, total)))
    return out.astype(jnp.int32)


def exchange_kernel(
    na, ne, green, pack,
    data, kron, terms,
    left_cc, right_cc, pack_n, hl, hr, rc, rh, to_r, to_l, forward, shifts, tables, spread, send, recv,
):
    p = lax.axis_index("atom")
    q = lax.axis_index("energy")
    up, down = p < na - 1, p > 0
    right, left = q < ne - 1, q > 0
    where_to = {(0, 1): right, (0, -1): left, (1, 0): up, (-1, 0): down}

    def peer(da, de):
        return {"atom": p + da, "energy": q + de}

    barrier = pltpu.get_barrier_semaphore()
    for (da, de), there in where_to.items():
        @pl.when(there)
        def _(da=da, de=de):
            pl.semaphore_signal(barrier, inc=1, device_id=peer(da, de), device_id_type=MESH)

    low = lax.broadcasted_iota(jnp.int32, (2 * SQ, E_DEV), 1) < 64

    def mix(a, b):
        return jnp.where(low, a, b).astype(BF16)

    def far_atom(c):
        return c + 6 if c < 2 else c + 2

    for c in range(4):
        near = green[c].astype(F32)
        far = pltpu.roll(green[far_atom(c)].astype(F32), 64, 1)
        to_r[c] = mix(far, near)
        to_l[c] = mix(near, far)

    def clear(ref):
        ref[...] = jnp.zeros(ref.shape, ref.dtype)

    @pl.when(jnp.logical_not(left))
    def _():
        clear(hl)

    @pl.when(jnp.logical_not(right))
    def _():
        clear(hr)

    for side, there in ((0, down), (1, up)):
        @pl.when(jnp.logical_not(there))
        def _(side=side):
            clear(rc.at[pl.ds(2 * side, 2)])
            clear(rh.at[pl.ds(2 * side, 2)])
            clear(pack_n.at[side])

    slots = iter(range(16))

    def copy_to(source, target, da, de):
        i = next(slots)
        copy = pltpu.make_async_remote_copy(
            src_ref=source,
            dst_ref=target,
            send_sem=send.at[i],
            recv_sem=recv.at[i],
            device_id=peer(da, de),
            device_id_type=MESH,
        )
        return copy, where_to[da, de], where_to[-da, -de]

    def start(items):
        for copy, sends, _ in items:
            pl.when(sends)(copy.start)

    def arrive(items):
        for copy, _, gets in items:
            pl.when(gets)(copy.wait_recv)

    def sent(items):
        for copy, sends, _ in items:
            pl.when(sends)(copy.wait_send)

    halos = [
        [copy_to(to_r.at[c], hl.at[c], 0, 1), copy_to(to_l.at[c], hr.at[c], 0, -1)] for c in range(4)
    ]
    small = [
        copy_to(pack, pack_n.at[0], 1, 0),
        copy_to(pack, pack_n.at[1], -1, 0),
    ]
    rims = [
        copy_to(green.at[pl.ds(6, 2)], rc.at[pl.ds(0, 2)], 1, 0),
        copy_to(green.at[pl.ds(0, 2)], rc.at[pl.ds(2, 2)], -1, 0),
    ]
    passed = [
        copy_to(forward.at[pl.ds(0, 2)], rh.at[pl.ds(0, 2)], 1, 0),
        copy_to(forward.at[pl.ds(2, 2)], rh.at[pl.ds(2, 2)], -1, 0),
    ]

    pl.semaphore_wait(barrier, sum(there.astype(jnp.int32) for there in where_to.values()))
    start(halos[0])
    start(halos[1])
    start(small)
    start(rims)

    row = lax.broadcasted_iota(jnp.int32, (2 * E_DEV, E_DEV), 0)
    col = lax.broadcasted_iota(jnp.int32, (2 * E_DEV, E_DEV), 1)
    outer = row - E_DEV
    for kind in range(2):
        if kind == 0:
            energy = jnp.where(outer < 64, outer + 128, outer - 128)
        else:
            energy = jnp.where(outer < 64, outer - 64, outer + 64)
        delta = (jnp.where(row < E_DEV, row, energy) - col).astype(F32)
        for m in range(MODES):
            n, k = pack[SLOTS + 3 : SLOTS + 4, m : m + 1], pack[SLOTS + 4 : SLOTS + 5, m : m + 1]
            value = jnp.where(delta == -k, n, jnp.where(delta == k, n + 1.0, 0.0))
            shifts[kind, m // 2, :, (m % 2) * 128 : (m % 2) * 128 + 128] = value.astype(BF16)

    def expand(source, table, target):
        rows = jnp.concatenate(
            [source[0:SLOTS, m * SQ : (m + 1) * SQ] for m in range(MODES)], axis=0
        ).astype(BF16)
        wide = jnp.dot(rows, tables[table], preferred_element_type=F32)
        for m in range(MODES):
            for i in range(NORB):
                target[m, i * SLOTS : (i + 1) * SLOTS, :] = wide[
                    m * SLOTS : (m + 1) * SLOTS, i * 128 : (i + 1) * 128
                ]

    for group in range(4):
        right_cc[group, :, NORB * SLOTS :, :] = jnp.zeros((MODES, 256 - NORB * SLOTS, 128), F32)
    fill_tables(tables)
    spread[...] = spread_matrix()
    expand(pack, 0, left_cc.at[0])
    expand(pack, 1, right_cc.at[0])
    expand(pack, 2, left_cc.at[1])
    expand(pack, 3, right_cc.at[1])

    def build(group, s):
        for m in range(MODES):
            right = right_cc[group, m, pl.ds(s, PADROW, stride=SLOTS), :]
            for i in range(NORB):
                left = left_cc[group, m, pl.ds(i * SLOTS + s, 1), :]
                kron[group * SLOTS + s, i * PADROW : (i + 1) * PADROW, m * 128 : (m + 1) * 128] = (
                    left * right
                ).astype(BF16)

    def build_first(s, carry):
        build(0, s)
        return carry

    def build_second(s, carry):
        build(1, s)
        return carry

    def build_neighbours(s, carry):
        build(2, s)
        build(3, s)
        return carry

    lax.fori_loop(0, SLOTS, build_first, 0)
    sent(halos[0])
    start(halos[2])
    lax.fori_loop(0, SLOTS, build_second, 0)
    arrive(small)
    for side in range(2):
        expand(pack_n.at[side], 2, left_cc.at[2 + side])
        expand(pack_n.at[side], 3, right_cc.at[2 + side])

    heads = [ref[SLOTS : SLOTS + 8, 0:128] for ref in (pack, pack_n.at[0], pack_n.at[1])]
    terms[...] = term_list(*heads, (p * ATOMS_DEV).astype(F32))

    def shift(d, kind, centre, halo):
        wide = jnp.concatenate([centre, halo], axis=1)
        rows = jnp.dot(spread[...], wide, preferred_element_type=F32).astype(BF16)
        for pair in range(MODES // 2):
            both = jnp.dot(rows, shifts[kind, pair], preferred_element_type=F32).astype(BF16)
            for half in range(2):
                at = (2 * pair + half) * 128
                for part in range(2):
                    data[d, at : at + 128, part * 128 : part * 128 + 128] = both[
                        part * 128 : part * 128 + 128, half * 128 : half * 128 + 128
                    ]

    def own_halos(c):
        lower, upper = hl[c].astype(F32), hr[c].astype(F32)
        return mix(upper, lower), mix(lower, upper)

    def shift_own(c, far):
        near_halo, far_halo = own_halos(c)
        shift(c, 0, green[c], near_halo)
        shift(6 + c, 1, green[far], far_halo)

    sent(halos[1])
    start(halos[3])
    arrive(halos[0])
    arrive(halos[1])
    for c in range(2):
        near_halo, far_halo = own_halos(c)
        forward[c] = far_halo
        forward[2 + c] = near_halo
    start(passed)
    lax.fori_loop(0, SLOTS, build_neighbours, 0)

    def first_half(c, carry):
        shift_own(c, c + 6)
        return carry

    lax.fori_loop(0, 2, first_half, 0)
    arrive(halos[2])
    shift_own(2, 4)
    arrive(rims)
    arrive(passed)

    def rim(c, carry):
        shift(4 + c, 0, rc[2 + c], rh[2 + c])
        shift(10 + c, 1, rc[c], rh[c])
        return carry

    lax.fori_loop(0, 2, rim, 0)
    arrive(halos[3])
    shift_own(3, 5)
    for items in halos[2:] + [small, rims, passed]:
        sent(items)


def exchange(na, ne, green, pack):
    vm = pl.BlockSpec(memory_space=pltpu.VMEM)
    slab = (2 * SQ, E_DEV)
    shape = jax.ShapeDtypeStruct
    return pl.pallas_call(
        functools.partial(exchange_kernel, na, ne),
        out_shape=[
            shape((ATOMS_DEV + 4, MODES * 128, 2 * E_DEV), BF16),
            shape((4 * SLOTS, KR, MODES * 128), BF16),
            shape((8, 128), jnp.int32),
        ],
        in_specs=[vm] * 2,
        out_specs=[vm] * 3,
        scratch_shapes=[
            pltpu.VMEM((4, MODES, 256, 128), F32),
            pltpu.VMEM((4, MODES, 256, 128), F32),
            pltpu.VMEM((2,) + pack.shape, F32),
            pltpu.VMEM((4,) + slab, BF16),
            pltpu.VMEM((4,) + slab, BF16),
            pltpu.VMEM((4,) + slab, BF16),
            pltpu.VMEM((4,) + slab, BF16),
            pltpu.VMEM((4,) + slab, BF16),
            pltpu.VMEM((4,) + slab, BF16),
            pltpu.VMEM((4,) + slab, BF16),
            pltpu.VMEM((2, MODES // 2, 2 * E_DEV, 256), BF16),
            pltpu.VMEM((4, SQ, NORB * 128), BF16),
            pltpu.VMEM((256, 2 * SQ), BF16),
            pltpu.SemaphoreType.DMA((16,)),
            pltpu.SemaphoreType.DMA((16,)),
        ],
        compiler_params=pltpu.CompilerParams(
            collective_id=0, has_side_effects=True, vmem_limit_bytes=14 * 2**20
        ),
        name="exchange",
    )(green, pack)


def born_kernel(terms, data, kron, out, acc, collect):
    total = terms[3, 0]
    acc[...] = jnp.zeros_like(acc)

    def visit(step, carry):
        for u in range(UNROLL):
            at = step * UNROLL + u
            t, d, o = terms[0, at], terms[1, at], terms[2, at]
            acc[o] += jnp.dot(kron[t], data[d], preferred_element_type=F32)
        return carry

    lax.fori_loop(0, lax.div(total + UNROLL - 1, UNROLL), visit, 0)

    collect[...] = collect_matrix()
    for o in range(0, ATOMS_DEV, 2):
        one, two = acc[o].astype(BF16), acc[o + 1].astype(BF16)
        tall = jnp.concatenate(
            [
                jnp.concatenate([one[:, :E_DEV], two[:, :E_DEV]], axis=1),
                jnp.concatenate([one[:, E_DEV:], two[:, E_DEV:]], axis=1),
            ],
            axis=0,
        )
        both = jnp.dot(collect[...], tall, preferred_element_type=F32).astype(BF16)
        out[o] = both[:, :E_DEV]
        out[o + 1] = both[:, E_DEV:]


def born(*arrays):
    vm = pl.BlockSpec(memory_space=pltpu.VMEM)
    return pl.pallas_call(
        born_kernel,
        out_shape=jax.ShapeDtypeStruct((ATOMS_DEV, 2 * SQ, E_DEV), BF16),
        in_specs=[pl.BlockSpec(memory_space=pltpu.SMEM)] + [vm] * 2,
        out_specs=vm,
        scratch_shapes=[
            pltpu.VMEM((ATOMS_DEV + 1, KR, 2 * E_DEV), F32),
            pltpu.VMEM((2 * SQ, 2 * KR), BF16),
        ],
        compiler_params=pltpu.CompilerParams(vmem_limit_bytes=6 * 2**20),
        name="born",
    )(*arrays)


def per_device(na, ne, green, coupling, pairs, counts, occupation, offsets):
    width = coupling.shape[1]
    row = lax.broadcasted_iota(jnp.int32, (SLOTS + 8, width), 0)
    pack = jnp.pad(coupling.astype(F32), ((0, 8), (0, 0)))
    for r, x in enumerate((pairs[:, 0], pairs[:, 1], counts, occupation, offsets)):
        line = jnp.pad(x.astype(F32), (0, width - x.shape[0]))
        pack = jnp.where(row == SLOTS + r, line[None, :], pack)
    data, kron, terms = exchange(na, ne, green, pack)
    return born(terms, data, kron)


def solution(mesh):
    placed = (P("atom", None, "energy"), P("atom", None), P("atom", None), P("atom"), P(), P())
    return jax.shard_map(
        functools.partial(per_device, mesh.shape["atom"], mesh.shape["energy"]),
        mesh=mesh,
        in_specs=placed,
        out_specs=P("atom", None, "energy"),
        check_vma=False,
    )
```

profile of v0, /device:TPU:0, one launch (start us, length us, event | category | flops | bytes accessed | tf_op | source)
XLA Modules:
  0.0 28.6 jit_solution(6677937059348467664)
XLA Ops:
  0.7 0.7 %convert_element_type.29 = f32[8]{0:T(128)S(1)} convert(s32[8]{0:T(128)} %param.11) | non-fusion elementwise | flops 8 | bytes 64 | tf_op jit(solution)/shard_map/convert_element_type | solution.py:406
  1.3 0.8 %convert_bitcast_fusion.1 = (f32[16]{0:T(128)S(1)}, f32[16]{0:T(128)S(1)}) fusion(s32[16,2]{0,1:T(2,128)} %param.8), kind=kLoop, calls=%fused_computation.3 | loop fusion | flops 32 | bytes 256 | tf_op jit(solution)/shard_map/convert_element_type | solution.py:406
  2.1 0.7 %pad.26 = f32[800]{0:T(1024)S(1)} pad(f32[8]{0:T(128)} %param.10, f32[]{:T(128)} %constant.3.clone.1), padding=0_792 | pad | bytes 3236 | tf_op jit(solution)/shard_map/jit(_pad)/pad | solution.py:406
  2.8 0.8 %select_select_fusion.pack = f32[24,800]{1,0:T(8,128)S(1)} fusion(bf16[16,800]{1,0:T(8,128)(2,1)} %param.7, f32[800]{0:T(1024)S(1)} %pad.29, f32[800]{0:T(1024)S(1)} %pad.28, f32[800]{0:T(1024)S(1)} %pad.27, f32[800]{0:T(1024)S(1)} %pad.26, f32[800]{0:T(1024)S(1)} %pad.25, pred[24]{0:T(512)(128)(4,1)S(1)} %get-tuple-element.13, ...), kind=kLoop, calls=%fused_computation | loop fusion | flops 115200 | bytes 118520 | tf_op jit(solution)/shard_map/jit(_where)/select_n | solution.py:407
  3.6 0.0 copy-start
  3.7 1.0 %copy-done = bf16[8,200,128]{2,1,0:T(8,128)(2,1)S(1)} copy-done((bf16[8,200,128]{2,1,0:T(8,128)(2,1)S(1)}, bf16[8,200,128]{2,1,0:T(8,128)(2,1)}, u32[]{:S(2)}) %copy-start) | copy-done | bytes 409624
  4.6 17.7 %exchange.1 = (bf16[12,1024,256]{2,1,0:T(8,128)(2,1)S(1)}, bf16[64,160,1024]{2,1,0:T(8,128)(2,1)S(1)}, s32[8,128]{1,0:T(8,128)S(1)}) custom-call(bf16[8,200,128]{2,1,0:T(8,128)(2,1)S(1)} %copy-done, f32[24,800]{1,0:T(8,128)S(1)} %select_select_fusion.pack), custom_call_target="tpu_custom_call" | custom-call | tf_op jit(solution)/shard_map/exchange/pallas_call | solution.py:324
  22.4 6.2 %born.1 = bf16[8,200,128]{2,1,0:T(8,128)(2,1)} custom-call(s32[8,128]{1,0:T(8,128)S(1)} %get-tuple-element.8.terms, bf16[12,1024,256]{2,1,0:T(8,128)(2,1)S(1)} %get-tuple-element.9.data, bf16[64,160,1024]{2,1,0:T(8,128)(2,1)S(1)} %get-tuple-element.10.kron), custom_call_target="tpu_custom_call" | custom-call | tf_op jit(solution)/shard_map/born/pallas_call | solution.py:387
  (7 shorter events, 0.0 us)
Async XLA Ops:
  3.6 1.0 %copy-start = (bf16[8,200,128]{2,1,0:T(8,128)(2,1)S(1)}, bf16[8,200,128]{2,1,0:T(8,128)(2,1)}, u32[]{:S(2)}) copy-start(bf16[8,200,128]{2,1,0:T(8,128)(2,1)} %green.1) | copy-start | bytes 1228804
where the time goes:
time: 28.1 us; the launch traced here: 28.6 us
  Pallas kernels  24 us (85%)
  other arithmetic  2.26 us (8%)
  local copies, waits for them, and re-layouts  1.68 us (6%)
  between operations  0.71 us (3%)
    pallas_call x1, Pallas kernels, exchange(): pl.pallas_call(functools.partial(exchange_kernel, na, ne), out_shape=[sha...  17.7 us
    pallas_call x1, Pallas kernels, born(): pl.pallas_call(born_kernel, out_shape=jax.ShapeDtypeStruct((ATOMS_DEV, 2...  6.23 us
    convert_element_type x2, other arithmetic, per_device(): line = jnp.pad(x.astype(F32), (0, width - x.shape[0]))  1.42 us
    unnamed x2, local copies, waits for them, and re-layouts  1 us
    select_n x1, other arithmetic, per_device(): pack = jnp.where(row == SLOTS + r, line[None, :], pack)  0.83 us
    pad x5, local copies, waits for them, and re-layouts, per_device(): line = jnp.pad(x.astype(F32), (0, width - x.shape[0]))  0.68 us

commit v1 on v0

--- a/solution.py
+++ b/solution.py
@@ -12,7 +12,7 @@
 KMAX = 64
 SQ = NORB * NORB
 PADROW = 16
-KR = NORB * PADROW
+KR = NORB * 8 + 2 * PADROW
 ATOMS_DEV = 8
 E_DEV = 128
 SLOTS = 16
@@ -50,12 +50,15 @@
     col = lax.broadcasted_iota(jnp.int32, (2 * SQ, 2 * KR), 1)
     part = jnp.where(col < KR, 0, 1)
     at = col - part * KR
-    i, l = lax.shift_right_logical(at, 4), at & (PADROW - 1)
-    return one_where((l < NORB) & (row == part * SQ + i * NORB + l))
+    late = at - NORB * 8
+    early = late < 0
+    i = jnp.where(early, lax.shift_right_logical(at, 3), late & (PADROW - 1))
+    l = jnp.where(early, at & 7, 8 + lax.shift_right_logical(jnp.maximum(late, 0), 4))
+    return one_where((i < NORB) & (row == part * SQ + i * NORB + l))
 
 
 def term_list(own, below, above, base):
-    lane = lax.broadcasted_iota(jnp.int32, (1, 128), 1).astype(F32)
+    lane = lax.broadcasted_iota(jnp.int32, (1, SLOTS), 1).astype(F32)
 
     def place(rel):
         inner = jnp.where((rel == 4) | (rel == 5), rel + 4, rel)
@@ -63,27 +66,27 @@
 
     entries = []
     for group, source in ((0, own), (2, below), (3, above)):
-        a, b = source[0:1] - base, source[1:2] - base
-        live = lane < source[2:3, 0:1]
+        a, b = source[0:1].astype(F32) - base, source[1:2].astype(F32) - base
+        live = lane < source[2:3].astype(F32)
         if group == 0:
             entries.append((live, lane, place(b), a))
             group = 1
         entries.append((live & (b >= 0) & (b < 8), group * SLOTS + lane, place(a), b))
 
     before = one_where(
-        lax.broadcasted_iota(jnp.int32, (128, 128), 0) < lax.broadcasted_iota(jnp.int32, (128, 128), 1)
+        lax.broadcasted_iota(jnp.int32, (SLOTS, SLOTS), 0) < lax.broadcasted_iota(jnp.int32, (SLOTS, SLOTS), 1)
     )
-    place_at = lax.broadcasted_iota(jnp.int32, (128, 128), 0).astype(F32)
+    place_at = lax.broadcasted_iota(jnp.int32, (128, SLOTS), 0).astype(F32)
     total = jnp.zeros((1, 1), F32)
-    tables = [jnp.zeros((128, 128), F32) for _ in range(3)]
+    tables = [jnp.zeros((128, SLOTS), F32) for _ in range(3)]
     for keep, *values in entries:
         flags = jnp.where(keep, 1.0, 0.0)
-        many = jnp.broadcast_to(flags, (8, 128)).astype(BF16)
+        many = jnp.broadcast_to(flags, (8, SLOTS)).astype(BF16)
         at = jnp.dot(many, before, preferred_element_type=F32)[0:1] + total
         total = total + jnp.sum(flags, axis=1, keepdims=True)
         chosen = jnp.where(place_at == at, 1.0, 0.0) * flags
         tables = [table + chosen * value for table, value in zip(tables, values)]
-    ones = jnp.ones((8, 128), BF16)
+    ones = jnp.ones((8, SLOTS), BF16)
     t, d, o = (
         lax.dot_general(ones, table.astype(BF16), (((1,), (1,)), ((), ())), preferred_element_type=F32)
         for table in tables
@@ -96,9 +99,9 @@
 
 
 def exchange_kernel(
-    na, ne, green, pack,
+    na, ne, green, pack, meta,
     data, kron, terms,
-    left_cc, right_cc, pack_n, hl, hr, rc, rh, to_r, to_l, forward, shifts, tables, spread, send, recv,
+    left_cc, right_cc, pack_n, meta_n, hl, hr, rc, rh, to_r, to_l, forward, shifts, tables, spread, send, recv,
 ):
     p = lax.axis_index("atom")
     q = lax.axis_index("energy")
@@ -146,6 +149,7 @@
             clear(rc.at[pl.ds(2 * side, 2)])
             clear(rh.at[pl.ds(2 * side, 2)])
             clear(pack_n.at[side])
+            clear(meta_n.at[side])
 
     slots = iter(range(16))
 
@@ -179,6 +183,8 @@
     small = [
         copy_to(pack, pack_n.at[0], 1, 0),
         copy_to(pack, pack_n.at[1], -1, 0),
+        copy_to(meta, meta_n.at[0], 1, 0),
+        copy_to(meta, meta_n.at[1], -1, 0),
     ]
     rims = [
         copy_to(green.at[pl.ds(6, 2)], rc.at[pl.ds(0, 2)], 1, 0),
@@ -205,7 +211,7 @@
             energy = jnp.where(outer < 64, outer - 64, outer + 64)
         delta = (jnp.where(row < E_DEV, row, energy) - col).astype(F32)
         for m in range(MODES):
-            n, k = pack[SLOTS + 3 : SLOTS + 4, m : m + 1], pack[SLOTS + 4 : SLOTS + 5, m : m + 1]
+            n, k = pack[SLOTS + m : SLOTS + m + 1, 0:1], pack[SLOTS + m : SLOTS + m + 1, 1:2]
             value = jnp.where(delta == -k, n, jnp.where(delta == k, n + 1.0, 0.0))
             shifts[kind, m // 2, :, (m % 2) * 128 : (m % 2) * 128 + 128] = value.astype(BF16)
 
@@ -221,7 +227,7 @@
                 ]
 
     for group in range(4):
-        right_cc[group, :, NORB * SLOTS :, :] = jnp.zeros((MODES, 256 - NORB * SLOTS, 128), F32)
+        left_cc[group, :, NORB * SLOTS :, :] = jnp.zeros((MODES, 256 - NORB * SLOTS, 128), F32)
     fill_tables(tables)
     spread[...] = spread_matrix()
     expand(pack, 0, left_cc.at[0])
@@ -231,12 +237,16 @@
 
     def build(group, s):
         for m in range(MODES):
-            right = right_cc[group, m, pl.ds(s, PADROW, stride=SLOTS), :]
-            for i in range(NORB):
-                left = left_cc[group, m, pl.ds(i * SLOTS + s, 1), :]
-                kron[group * SLOTS + s, i * PADROW : (i + 1) * PADROW, m * 128 : (m + 1) * 128] = (
-                    left * right
-                ).astype(BF16)
+            lanes = slice(m * 128, (m + 1) * 128)
+            right = right_cc[group, m, pl.ds(s, 8, stride=SLOTS), :]
+            left = left_cc[group, m, pl.ds(s, PADROW, stride=SLOTS), :]
+            for i in range(0, NORB, 2):
+                rows = [left_cc[group, m, pl.ds((i + n) * SLOTS + s, 1), :] * right for n in range(2)]
+                kron[group * SLOTS + s, i * 8 : i * 8 + 16, lanes] = jnp.concatenate(rows, axis=0).astype(BF16)
+            for l in range(8, NORB):
+                row = right_cc[group, m, pl.ds(l * SLOTS + s, 1), :]
+                at = NORB * 8 + (l - 8) * PADROW
+                kron[group * SLOTS + s, at : at + PADROW, lanes] = (row * left).astype(BF16)
 
     def build_first(s, carry):
         build(0, s)
@@ -260,7 +270,7 @@
         expand(pack_n.at[side], 2, left_cc.at[2 + side])
         expand(pack_n.at[side], 3, right_cc.at[2 + side])
 
-    heads = [ref[SLOTS : SLOTS + 8, 0:128] for ref in (pack, pack_n.at[0], pack_n.at[1])]
+    heads = [meta[...], meta_n[0], meta_n[1]]
     terms[...] = term_list(*heads, (p * ATOMS_DEV).astype(F32))
 
     def shift(d, kind, centre, halo):
@@ -317,7 +327,7 @@
         sent(items)
 
 
-def exchange(na, ne, green, pack):
+def exchange(na, ne, green, pack, meta):
     vm = pl.BlockSpec(memory_space=pltpu.VMEM)
     slab = (2 * SQ, E_DEV)
     shape = jax.ShapeDtypeStruct
@@ -328,12 +338,13 @@
             shape((4 * SLOTS, KR, MODES * 128), BF16),
             shape((8, 128), jnp.int32),
         ],
-        in_specs=[vm] * 2,
+        in_specs=[vm] * 3,
         out_specs=[vm] * 3,
         scratch_shapes=[
             pltpu.VMEM((4, MODES, 256, 128), F32),
             pltpu.VMEM((4, MODES, 256, 128), F32),
             pltpu.VMEM((2,) + pack.shape, F32),
+            pltpu.VMEM((2,) + meta.shape, jnp.int32),
             pltpu.VMEM((4,) + slab, BF16),
             pltpu.VMEM((4,) + slab, BF16),
             pltpu.VMEM((4,) + slab, BF16),
@@ -351,7 +362,7 @@
             collective_id=0, has_side_effects=True, vmem_limit_bytes=14 * 2**20
         ),
         name="exchange",
-    )(green, pack)
+    )(green, pack, meta)
 
 
 def born_kernel(terms, data, kron, out, acc, collect):
@@ -400,12 +411,11 @@
 
 def per_device(na, ne, green, coupling, pairs, counts, occupation, offsets):
     width = coupling.shape[1]
-    row = lax.broadcasted_iota(jnp.int32, (SLOTS + 8, width), 0)
-    pack = jnp.pad(coupling.astype(F32), ((0, 8), (0, 0)))
-    for r, x in enumerate((pairs[:, 0], pairs[:, 1], counts, occupation, offsets)):
-        line = jnp.pad(x.astype(F32), (0, width - x.shape[0]))
-        pack = jnp.where(row == SLOTS + r, line[None, :], pack)
-    data, kron, terms = exchange(na, ne, green, pack)
+    lane = lax.broadcasted_iota(jnp.int32, (MODES, width), 1)
+    modes = jnp.where(lane == 0, occupation[:, None], offsets.astype(F32)[:, None])
+    pack = jnp.concatenate([coupling.astype(F32), modes], axis=0)
+    meta = jnp.concatenate([pairs.T, jnp.broadcast_to(counts, (1, SLOTS))], axis=0)
+    data, kron, terms = exchange(na, ne, green, pack, meta)
     return born(terms, data, kron)
 
 

time: 28.1 us -> 27.2 us (0.968); the launches traced: 28.6 us -> 26.9 us
  Pallas kernels: 24 us -> 22.4 us
    pallas_call x1, Pallas kernels: 6.23 us -> 4.65 us  [born(): pl.pallas_call(born_kernel, out_shape=jax.ShapeDtypeStruct((ATOMS_DEV, 2...]
    concatenate x0 -> x1, local copies, waits for them, and re-layouts: none -> 0.68 us  [per_device(): jnp.concatenate([pairs.T, jnp.broadcast_to(counts, (1, SLOTS))], axis=0)]
    pad x5 -> x0, local copies, waits for them, and re-layouts: 0.68 us -> none  [per_device(): line = jnp.pad(x.astype(F32), (0, width - x.shape[0]))]
where the time goes in v1:
time: 27.2 us; the launch traced here: 26.9 us
  Pallas kernels  22.4 us (82%)
  other arithmetic  2.15 us (8%)
  local copies, waits for them, and re-layouts  1.68 us (6%)
  between operations  0.67 us (2%)
    pallas_call x1, Pallas kernels, exchange(): pl.pallas_call(functools.partial(exchange_kernel, na, ne), out_shape=[sha...  17.8 us
    pallas_call x1, Pallas kernels, born(): pl.pallas_call(born_kernel, out_shape=jax.ShapeDtypeStruct((ATOMS_DEV, 2...  4.65 us
    unnamed x2, local copies, waits for them, and re-layouts  1 us
    convert_element_type x1, other arithmetic, per_device(): pack = jnp.concatenate([coupling.astype(F32), modes], axis=0)  0.75 us
    select_n x1, other arithmetic, per_device(): jnp.where(lane == 0, occupation[:, None], offsets.astype(F32)[:, None])  0.73 us
    concatenate x1, local copies, waits for them, and re-layouts, per_device(): jnp.concatenate([pairs.T, jnp.broadcast_to(counts, (1, SLOTS))], axis=0)  0.68 us
    convert_element_type x1, other arithmetic, per_device(): offsets.astype(F32)[:, None]  0.66 us

profile of v1, /device:TPU:0, one launch (start us, length us, event | category | flops | bytes accessed | tf_op | source)
XLA Modules:
  0.0 26.9 jit_solution(13340984923243709286)
XLA Ops:
  0.7 0.7 %convert_element_type.7 = f32[8]{0:T(128)S(1)} convert(s32[8]{0:T(128)} %param.11) | non-fusion elementwise | flops 8 | bytes 64 | tf_op jit(solution)/shard_map/convert_element_type | solution.py:415
  1.3 0.7 %concatenate.7.meta = s32[3,16]{1,0:T(4,128)S(1)} pad(s32[2,16]{1,0:T(2,128)} %bitcast.3, s32[]{:T(128)} %bitcast.2), padding=0_1x0_0 | pad | bytes 324 | tf_op jit(solution)/shard_map/concatenate | solution.py:417
  2.0 0.7 %broadcast_select_fusion = f32[8,800]{1,0:T(8,128)S(1)} fusion(f32[8]{0:T(128)S(1)} %convert_element_type.7, f32[8]{0:T(128)} %param.10, pred[800]{0:T(1024)(128)(4,1)S(1)} %iota_compare_fusion), kind=kLoop, calls=%fused_computation.1 | loop fusion | flops 6400 | bytes 26464 | tf_op jit(solution)/shard_map/jit(_where)/select_n | solution.py:415
  2.7 0.8 %convert_element_type.6 = f32[16,800]{1,0:T(8,128)S(1)} convert(bf16[16,800]{1,0:T(8,128)(2,1)} %param.7) | non-fusion elementwise | flops 12800 | bytes 76800 | tf_op jit(solution)/shard_map/convert_element_type | solution.py:416
  3.5 0.0 copy-start
  3.5 1.0 %copy-done = bf16[8,200,128]{2,1,0:T(8,128)(2,1)S(1)} copy-done((bf16[8,200,128]{2,1,0:T(8,128)(2,1)S(1)}, bf16[8,200,128]{2,1,0:T(8,128)(2,1)}, u32[]{:S(2)}) %copy-start) | copy-done | bytes 409624
  4.5 17.8 %exchange.1 = (bf16[12,1024,256]{2,1,0:T(8,128)(2,1)S(1)}, bf16[64,112,1024]{2,1,0:T(8,128)(2,1)S(1)}, s32[8,128]{1,0:T(8,128)S(1)}) custom-call(bf16[8,200,128]{2,1,0:T(8,128)(2,1)S(1)} %copy-done, f32[24,800]{1,0:T(8,128)S(1)} %pad_maximum_fusion.pack, s32[3,16]{1,0:T(4,128)S(1)} %concatenate.7.meta), custom_call_target="tpu_custom_call" | custom-call | tf_op jit(solution)/shard_map/exchange/pallas_call | solution.py:334
  22.3 4.6 %born.1 = bf16[8,200,128]{2,1,0:T(8,128)(2,1)} custom-call(s32[8,128]{1,0:T(8,128)S(1)} %get-tuple-element.8.terms, bf16[12,1024,256]{2,1,0:T(8,128)(2,1)S(1)} %get-tuple-element.9.data, bf16[64,112,1024]{2,1,0:T(8,128)(2,1)S(1)} %get-tuple-element.10.kron), custom_call_target="tpu_custom_call" | custom-call | tf_op jit(solution)/shard_map/born/pallas_call | solution.py:398
  (2 shorter events, 0.0 us)
Async XLA Ops:
  3.5 1.0 %copy-start = (bf16[8,200,128]{2,1,0:T(8,128)(2,1)S(1)}, bf16[8,200,128]{2,1,0:T(8,128)(2,1)}, u32[]{:S(2)}) copy-start(bf16[8,200,128]{2,1,0:T(8,128)(2,1)} %green.1) | copy-start | bytes 1228804
